TPU v7x, 32 devices: a whole 2x2x4 slice. The times are simulated.
32 devices in a mesh: groups: 2 (over y), ctx: 4 (over z), mp: 4 (over x, core).
Axes of the slice: x: 2, y: 2, z: 4, core: 2. Of those that a mesh axis runs over, the one named last changes fastest.
Arguments:
- features: bfloat16 [4, 512, 1536], P('groups', 'ctx'), parts along dimension 0, may hold values from -6 to 6
- frame_counts: int32 [4], P('groups'), parts along dimension 0, may hold values from 1 to 512, 768 in all
- attn_gain: float32 [1536], replicated, may hold values from 0.25 to 1.75
- w_qkv: bfloat16 [3, 1536, 1024], P(None, None, 'mp'), may hold values from -2 to 2
- w_out: bfloat16 [1024, 1536], P('mp'), may hold values from -0.375 to 0.375
- conv_gain: float32 [1536], replicated, may hold values from 0.25 to 1.75
- w_glu: bfloat16 [2, 1536, 1536], P(None, None, 'mp'), may hold values from -0.15625 to 0.15625
- kernel: float32 [31, 1536], P(None, 'mp'), may hold values from -2 to 2
- bn_scale: float32 [1536], P('mp'), may hold values from 0.5 to 2
- bn_shift: float32 [1536], P('mp'), may hold values from -2.5 to 2.5
- w_pw: bfloat16 [1536, 1536], P('mp'), may hold values from -0.15625 to 0.15625
- clip_level: int32 [1536], replicated, may hold values from 6 to 39
Outputs:
- encoded: bfloat16 [4, 512, 1536], P('groups', ('ctx', 'mp')), parts along dimension 0
There are 2 independent parts, one for each index of `groups`. A program takes and returns all parts, laid end to end along the dimension named above; an argument that names none is the same for every part. Nothing has to cross between parts.
Inputs may be any that keep to these rules, and one draw needn't show every extreme that they name: frame_counts[s] frames of recording s fill slots 0 to frame_counts[s] - 1, later slots are padding; some recording fills all 512 slots.
All inputs are finite; a program needn't handle non-finite values.
Results may differ from a plain program's by a relative error of at most 0.023.
Values may be sent and summed in bfloat16 or wider, within the bound.
A program may use at most 128 MiB of HBM per device.

v0:
```python
import functools

import jax
import jax.numpy as jnp
from jax import lax
from jax.experimental import pallas as pl
from jax.experimental.pallas import tpu as pltpu
from jax.sharding import PartitionSpec as P

MESH = pl.DeviceIdType.MESH
HEAD_DIM = 64
LANES = 128
RIM = 16
W_CHUNKS = 2
epsilon = 1e-05
masked_score = -1e30
f32 = jnp.float32
bf16 = jnp.bfloat16


def loop(count, step):
    if count <= 2:
        for i in range(count):
            step(i)
    else:
        lax.fori_loop(0, count, lambda i, carry: (step(i), carry)[1], 0)


def when(cond):
    if cond is True:
        return lambda f: f()
    return lambda f: pl.when(cond)(lambda: f())


def normalise(values, gain):
    centred = values - jnp.mean(values, axis=-1, keepdims=True)
    variance = jnp.mean(centred * centred, axis=-1, keepdims=True)
    return (centred * lax.rsqrt(variance + epsilon) * gain).astype(bf16)


def fused(
    n, nx, ng, recs, frames, taps,
    feat_h, counts_h, ag_h, wqkv_h, wout_h, cg_h, wglu_h, ker_h, bns_h, bnb_h, wpw_h, clip_h, out,
    feat, counts, ag, cg, ker, bns, bnb, clip,
    wqkv, wo, wglu, wpw, xn, qkv_s, qkv_r, atto, att_all, w_s, tot_s, parts, sibs, res, gb, gp, halo, act,
    p5, s5, sum5, x5,
    ld, sm, qs, qr, wos, wor, ys, yr, zs, zr, fs, fr, ss, sr, hs, hr, bs, br, es, er,
):
    c = lax.axis_index("ctx")
    m = lax.axis_index("mp")
    x = lax.div(m, 2)
    core = lax.rem(m, 2)
    g_rank = lax.axis_index("groups")
    sibling = {"mp": x * 2 + (1 - core)}
    rows, width = feat.shape
    pairs = wqkv.shape[2] // LANES
    units = recs * pairs
    chans = gb.shape[2]
    rm = frames // (2 * nx)
    group = min(recs, 2)
    block = group * frames

    def ctx_at(k):
        return lax.rem(c + k, n)

    def has_unit(rank):
        return True if units == n else rank < units

    def x_peer(k):
        return {"mp": lax.rem(x + k, nx) * 2 + core}

    def y_peer(k):
        return {"groups": lax.rem(g_rank + k, ng)}

    def remote(src, dst, send, recv, where):
        return pltpu.make_async_remote_copy(
            src_ref=src, dst_ref=dst, send_sem=send, recv_sem=recv, device_id=where, device_id_type=MESH
        )

    barrier = pltpu.get_barrier_semaphore()
    for k in range(1, n):
        pl.semaphore_signal(barrier, inc=1, device_id={"ctx": ctx_at(k)}, device_id_type=MESH)
    for k in range(1, nx):
        pl.semaphore_signal(barrier, inc=1, device_id=x_peer(k), device_id_type=MESH)
    for k in range(1, ng):
        pl.semaphore_signal(barrier, inc=1, device_id=y_peer(k), device_id_type=MESH)
    pl.semaphore_signal(barrier, inc=1, device_id=sibling, device_id_type=MESH)

    pairs_in = [(feat_h, feat), (ag_h, ag), (counts_h, counts), (cg_h, cg), (ker_h, ker), (bns_h, bns),
                (bnb_h, bnb), (clip_h, clip)]
    smalls = [pltpu.make_async_copy(src, dst, sm.at[i]) for i, (src, dst) in enumerate(pairs_in)]
    loads = [pltpu.make_async_copy(wqkv_h.at[i], wqkv.at[i], ld.at[i]) for i in range(3)]
    loads.append(pltpu.make_async_copy(wglu_h, wglu, ld.at[3]))
    loads.append(pltpu.make_async_copy(wpw_h, wpw, ld.at[4]))
    loads.append(pltpu.make_async_copy(wout_h, wo.at[x], ld.at[5]))
    smalls[0].start()
    smalls[1].start()
    for i in (1, 0, 2):
        loads[i].start()
    for copy in smalls[2:]:
        copy.start()
    for i in (5, 3, 4):
        loads[i].start()
    smalls[0].wait()
    smalls[1].wait()

    gain = ag[...].reshape(1, width)

    def norm_in(i):
        at = pl.ds(pl.multiple_of(i * 32, 32), 32)
        xn[at, :] = normalise(feat[at, :].astype(f32), gain)

    lax.fori_loop(0, rows // 32, lambda i, carry: (norm_in(i), carry)[1], 0, unroll=4)

    pl.semaphore_wait(barrier, n - 1 + nx - 1 + ng - 1 + 1)

    local = wo.shape[1]
    share = local // ng
    sub = share // W_CHUNKS

    def w_rows(rank, chunk):
        return pl.ds(pl.multiple_of(rank * share + chunk * sub, sub), sub)

    w_copies = {}
    for chunk in range(W_CHUNKS):
        for k in range(1, nx):
            at = w_rows(g_rank, chunk)
            copy = remote(wout_h.at[at, :], wo.at[x, at, :], wos.at[k, chunk], wor.at[k, chunk], x_peer(k))
            copy.start()
            w_copies[k, chunk] = copy
    y_copies = []

    def hand_on(chunk):
        for k in range(1, nx):
            w_copies[k, chunk].wait_recv()
            at = w_rows(g_rank, chunk)
            held = wo.at[lax.rem(x - k + nx, nx), at, :]
            for j in range(1, ng):
                copy = remote(held, held, ys.at[k, chunk, j], yr.at[k, chunk, j], y_peer(j))
                copy.start()
                y_copies.append(copy)

    q_copies = []
    for i in (1, 0, 2):
        loads[i].wait()

        def project(g, i=i):
            at = pl.ds(pl.multiple_of(g * block, block), block)
            made = jnp.dot(xn[at, :], wqkv[i], preferred_element_type=f32).astype(bf16)
            for r in range(group):
                for p in range(pairs):
                    piece = made[r * frames : (r + 1) * frames, p * LANES : (p + 1) * LANES]
                    qkv_s[(g * group + r) * pairs + p, i] = piece

        loop(recs // group, project)
        for k in range(1, n):
            dest = ctx_at(k)
            copy = remote(
                qkv_s.at[lax.rem(dest, units), i], qkv_r.at[c, i], qs.at[i, k], qr.at[i, k], {"ctx": dest}
            )
            when(has_unit(dest))(copy.start)
            q_copies.append((copy, dest, i))

        @when(has_unit(c))
        def _(i=i):
            qkv_r[c, i] = qkv_s[lax.rem(c, units), i]

    z_copies = [
        remote(atto.at[k], att_all.at[x, lax.rem(c, units)], zs.at[k], zr.at[k], {"ctx": ctx_at(k)})
        for k in range(1, n)
    ]

    hand_on(0)
    smalls[2].wait()

    def arrived(which):
        @when(has_unit(c))
        def _():
            for copy, _dest, i in q_copies:
                if i in which:
                    copy.wait_recv()

    arrived((1, 0))
    own_rec = lax.div(lax.rem(c, units), pairs)
    live_keys = counts[own_rec]
    key_count = n * frames
    lane = lax.broadcasted_iota(jnp.int32, (1, LANES), 1)
    low = lane < HEAD_DIM
    seen = lax.broadcasted_iota(jnp.int32, (1, key_count), 1) < live_keys
    slots = w_s.shape[0]

    def weigh(k0, slot):
        keys = qkv_r[:, 1].reshape(key_count, LANES)
        queries = jnp.concatenate([qkv_r[ctx_at(k0), 0], qkv_r[ctx_at(k0 + 1), 0]], axis=0)
        for h in range(2):
            mine = jnp.where(low if h == 0 else jnp.logical_not(low), queries, jnp.zeros((), bf16))
            scores = lax.dot_general(mine, keys, (((1,), (1,)), ((), ())), preferred_element_type=f32)
            scores = jnp.where(seen, scores, masked_score)
            top = jnp.max(scores, axis=-1, keepdims=True)
            weights = jnp.exp((scores - top) * (HEAD_DIM**-0.5))
            tot_s[slot, h] = jnp.sum(weights, axis=-1, keepdims=True)
            w_s[slot, h] = weights.astype(bf16)

    def mix(k0, slot):
        values = qkv_r[:, 2].reshape(key_count, LANES)
        heads = [
            jnp.dot(w_s[slot, h], values, preferred_element_type=f32) / tot_s[slot, h] for h in range(2)
        ]
        both = jnp.where(low, heads[0], heads[1]).astype(bf16)
        atto[k0] = both[:frames]
        atto[k0 + 1] = both[frames:]

    def give(k):
        if k == 0:
            att_all[x, lax.rem(c, units)] = atto[0]
        else:
            z_copies[k - 1].start()

    starts = list(range(0, n, 2))
    if slots > 1:
        @when(has_unit(c))
        def _():
            for slot, k0 in enumerate(starts):
                weigh(k0, slot)

    for chunk in range(1, W_CHUNKS):
        hand_on(chunk)
    arrived((2,))

    @when(has_unit(c))
    def _():
        if slots > 1:
            for slot, k0 in reversed(list(enumerate(starts))):
                mix(k0, slot)
                give(k0 + 1)
                give(k0)
        else:
            def whole_step(i, carry):
                weigh(2 * i, 0)
                mix(2 * i, 0)
                return carry

            lax.fori_loop(0, n // 2, whole_step, 0)
            for k in range(n):
                give(k)

    f_copies = []
    for k in range(n):
        unit = lax.rem(c - k + n, n)
        spot = lax.rem(unit, units)

        @when(has_unit(unit))
        def _(k=k, unit=unit, spot=spot):
            if k > 0:
                remote(atto.at[k], att_all.at[x, spot], zs.at[k], zr.at[k], {"ctx": unit}).wait_recv()
            for j in range(1, nx):
                remote(
                    att_all.at[x, spot], att_all.at[x, spot], fs.at[j, k], fr.at[j, k], x_peer(j)
                ).start()

        for j in range(1, nx):
            f_copies.append(
                (remote(att_all.at[x, spot], att_all.at[x, spot], fs.at[j, k], fr.at[j, k], x_peer(j)), unit)
            )

    loads[5].wait()
    for copy in y_copies:
        copy.wait_recv()
    for copy, unit in f_copies:
        when(has_unit(unit))(copy.wait_recv)

    s_copies = []
    for rec in range(recs):
        gathered = jnp.concatenate(
            [att_all[i, rec * pairs + p] for i in range(nx) for p in range(pairs)], axis=1
        )
        parts[rec] = jnp.dot(
            gathered, wo[...].reshape(nx * pairs * LANES, width), preferred_element_type=f32
        ).astype(bf16)
        copy = remote(parts.at[rec], sibs.at[rec], ss.at[rec], sr.at[rec], sibling)
        copy.start()
        s_copies.append(copy)

    smalls[3].wait()
    conv_gain = cg[...].reshape(1, width)
    for rec in range(recs):
        s_copies[rec].wait_recv()

        def norm_conv(i, rec=rec):
            near = pl.ds(pl.multiple_of(i * 32, 32), 32)
            at = pl.ds(pl.multiple_of(rec * frames + i * 32, 32), 32)
            total = feat[at, :].astype(f32) + (parts[rec, near, :].astype(f32) + sibs[rec, near, :].astype(f32))
            res[at, :] = total
            xn[at, :] = normalise(total, conv_gain)

        lax.fori_loop(0, frames // 32, lambda i, carry: (norm_conv(i), carry)[1], 0, unroll=4)

    loads[3].wait()
    first_frame = c * frames
    frame_ids = first_frame + lax.broadcasted_iota(jnp.int32, (frames, 1), 0)

    def gate(g):
        at = pl.ds(pl.multiple_of(g * block, block), block)
        value_half = jnp.dot(xn[at, :], wglu[0], preferred_element_type=f32)
        gate_half = jnp.dot(xn[at, :], wglu[1], preferred_element_type=f32)
        gated = value_half * jax.nn.sigmoid(gate_half)
        for r in range(group):
            rec = g * group + r
            kept = jnp.where(frame_ids < counts[rec], gated[r * frames : (r + 1) * frames], 0.0).astype(bf16)
            gb[rec] = kept
            gp[rec, RIM : RIM + frames, :] = kept.astype(f32)

    loop(recs // group, gate)

    def up():
        return remote(gb.at[:, frames - RIM : frames, :], halo.at[0], hs.at[0], hr.at[0], {"ctx": lax.rem(c + 1, n)})

    def down():
        return remote(gb.at[:, 0:RIM, :], halo.at[1], hs.at[1], hr.at[1], {"ctx": lax.rem(c + n - 1, n)})

    @pl.when(c < n - 1)
    def _():
        up().start()

    @pl.when(c > 0)
    def _():
        down().start()

    for copy in smalls[4:]:
        copy.wait()
    scale = bns[...].reshape(1, chans)
    shift = bnb[...].reshape(1, chans)

    def depthwise(rec, start, count):
        for lo in range(0, chans, LANES):
            hi = min(lo + LANES, chans)
            total = jnp.zeros((count, hi - lo), f32)
            for tap in range(taps):
                begin = start + tap + RIM - taps // 2
                total = total + gp[rec, begin : begin + count, lo:hi] * ker[tap : tap + 1, lo:hi]
            v = total * scale[:, lo:hi] + shift[:, lo:hi]
            act[rec, start : start + count, lo:hi] = (v * jax.nn.sigmoid(v)).astype(bf16)

    def rim():
        @pl.when(c > 0)
        def _():
            up().wait_recv()

        @pl.when(c == 0)
        def _():
            halo[0] = jnp.zeros(halo.shape[1:], bf16)

        @pl.when(c < n - 1)
        def _():
            down().wait_recv()

        @pl.when(c == n - 1)
        def _():
            halo[1] = jnp.zeros(halo.shape[1:], bf16)

    b_copies = []
    e_copies = []

    def pass_on(rec):
        b_copies[rec].wait_recv()
        for i in range(nx):
            sum5[rec, i] = (p5[rec, i, core].astype(f32) + s5[rec, i].astype(f32)).astype(bf16)
        for k in range(1, nx):
            copy = remote(sum5.at[rec, lax.rem(x + k, nx)], x5.at[rec, k], es.at[rec, k], er.at[rec, k], x_peer(k))
            copy.start()
            e_copies.append(copy)

    for rec in range(recs):
        depthwise(rec, RIM, frames - 2 * RIM)
        if rec == 0:
            rim()
            loads[4].wait()
        gp[rec, 0:RIM, :] = halo[0, rec].astype(f32)
        gp[rec, RIM + frames : 2 * RIM + frames, :] = halo[1, rec].astype(f32)
        depthwise(rec, 0, RIM)
        depthwise(rec, frames - RIM, RIM)
        if rec > 0:
            pass_on(rec - 1)
        made = jnp.dot(act[rec], wpw[...], preferred_element_type=f32)
        p5[rec] = made.reshape(nx, 2, rm, width).astype(bf16)
        copy = remote(p5.at[rec, :, 1 - core], s5.at[rec], bs.at[rec], br.at[rec], sibling)
        copy.start()
        b_copies.append(copy)
    pass_on(recs - 1)

    row_start = pl.multiple_of(m * rm, rm)
    mine_ids = first_frame + row_start + lax.broadcasted_iota(jnp.int32, (rm, 1), 0)
    bound = clip[...].reshape(1, width).astype(f32) / 16.0
    for rec in range(recs):
        for k in range(1, nx):
            e_copies[rec * (nx - 1) + k - 1].wait_recv()
        at = pl.ds(pl.multiple_of(rec * frames + row_start, rm), rm)
        total = res[at, :] + sum5[rec, x].astype(f32)
        for k in range(1, nx):
            total = total + x5[rec, k].astype(f32)
        clipped = jnp.minimum(jnp.maximum(total, -bound), bound)
        out[rec] = jnp.where(mine_ids < counts[rec], clipped, 0.0).astype(bf16)

    for copy, dest, _i in q_copies:
        when(has_unit(dest))(copy.wait_send)

    @when(has_unit(c))
    def _():
        for copy in z_copies:
            copy.wait_send()

    for copy, unit in f_copies:
        when(has_unit(unit))(copy.wait_send)
    for copy in list(w_copies.values()) + y_copies + s_copies + b_copies + e_copies:
        copy.wait_send()

    @pl.when(c < n - 1)
    def _():
        up().wait_send()

    @pl.when(c > 0)
    def _():
        down().wait_send()


def shards(n, mp, ng, features, frame_counts, attn_gain, w_qkv, w_out, conv_gain, w_glu, kernel, bn_scale, bn_shift, w_pw, clip_level):
    recs, frames, width = features.shape
    nx = mp // 2
    rows = recs * frames
    local = w_qkv.shape[2]
    units = recs * local // LANES
    chans = w_glu.shape[2]
    rm = frames // mp
    taps = kernel.shape[0]
    vmem = pl.BlockSpec(memory_space=pltpu.VMEM)
    hbm = pl.BlockSpec(memory_space=pl.ANY)
    dma = pltpu.SemaphoreType.DMA
    slots = n // 2 if n <= 4 else 1
    scratch = [
        pltpu.VMEM((rows, width), bf16),
        pltpu.SMEM(frame_counts.shape, jnp.int32),
        pltpu.VMEM(attn_gain.shape, f32),
        pltpu.VMEM(conv_gain.shape, f32),
        pltpu.VMEM(kernel.shape, f32),
        pltpu.VMEM(bn_scale.shape, f32),
        pltpu.VMEM(bn_shift.shape, f32),
        pltpu.VMEM(clip_level.shape, jnp.int32),
        pltpu.VMEM(w_qkv.shape, bf16),
        pltpu.VMEM((nx, local, width), bf16),
        pltpu.VMEM(w_glu.shape, bf16),
        pltpu.VMEM(w_pw.shape, bf16),
        pltpu.VMEM((rows, width), bf16),
        pltpu.VMEM((units, 3, frames, LANES), bf16),
        pltpu.VMEM((n, 3, frames, LANES), bf16),
        pltpu.VMEM((n, frames, LANES), bf16),
        pltpu.VMEM((nx, units, frames, LANES), bf16),
        pltpu.VMEM((slots, 2, 2 * frames, n * frames), bf16),
        pltpu.VMEM((slots, 2, 2 * frames, 1), f32),
        pltpu.VMEM((recs, frames, width), bf16),
        pltpu.VMEM((recs, frames, width), bf16),
        pltpu.VMEM((rows, width), f32),
        pltpu.VMEM((recs, frames, chans), bf16),
        pltpu.VMEM((recs, frames + 2 * RIM, chans), f32),
        pltpu.VMEM((2, recs, RIM, chans), bf16),
        pltpu.VMEM((recs, frames, chans), bf16),
        pltpu.VMEM((recs, nx, 2, rm, width), bf16),
        pltpu.VMEM((recs, nx, rm, width), bf16),
        pltpu.VMEM((recs, nx, rm, width), bf16),
        pltpu.VMEM((recs, nx, rm, width), bf16),
        dma((6,)),
        dma((8,)),
        dma((3, n)), dma((3, n)),
        dma((nx, W_CHUNKS)), dma((nx, W_CHUNKS)),
        dma((nx, W_CHUNKS, ng)), dma((nx, W_CHUNKS, ng)),
        dma((n,)), dma((n,)),
        dma((nx, n)), dma((nx, n)),
        dma((recs,)), dma((recs,)),
        dma((2,)), dma((2,)),
        dma((recs,)), dma((recs,)),
        dma((recs, nx)), dma((recs, nx)),
    ]
    return pl.pallas_call(
        functools.partial(fused, n, nx, ng, recs, frames, taps),
        out_shape=jax.ShapeDtypeStruct((recs, rm, width), bf16),
        in_specs=[hbm] * 12,
        out_specs=vmem,
        scratch_shapes=scratch,
        compiler_params=pltpu.CompilerParams(
            collective_id=0, has_side_effects=True, vmem_limit_bytes=56 * 2**20
        ),
    )(
        features.reshape(rows, width), frame_counts, attn_gain, w_qkv, w_out, conv_gain, w_glu, kernel,
        bn_scale, bn_shift, w_pw, clip_level,
    )


def solution(mesh):
    return jax.shard_map(
        functools.partial(shards, mesh.shape["ctx"], mesh.shape["mp"], mesh.shape["groups"]),
        mesh=mesh,
        in_specs=(
            P("groups", "ctx", None),
            P("groups"),
            P(),
            P(None, None, "mp"),
            P("mp", None),
            P(),
            P(None, None, "mp"),
            P(None, "mp"),
            P("mp"),
            P("mp"),
            P("mp", None),
            P(),
        ),
        out_specs=P("groups", ("ctx", "mp"), None),
        check_vma=False,
    )
```

profile of v0, /device:TPU:0, one launch (start us, length us, event | category | flops | bytes accessed | tf_op | source)
XLA Modules:
  0.0 40.1 jit_solution(3115286639837237469)
XLA Ops:
  0.0 38.5 %shard_map.118 = bf16[2,32,1536]{2,1,0:T(8,128)(2,1)} custom-call(bf16[256,1536]{1,0:T(8,128)(2,1)} %bitcast.1, s32[2]{0:T(128)} %counts_h.1, f32[1536]{0:T(1024)} %ag_h.1, bf16[3,1536,256]{2,1,0:T(8,128)(2,1)} %wqkv_h.1, bf16[256,1536]{1,0:T(8,128)(2,1)} %wout_h.1, f32[1536]{0:T(1024)} %cg_h.1, bf16[2,1536,384]{2,1,0:T(8,128)(2,1)} %wglu_h.1, ...), custom_call_target="tpu_custom_call" | custom-call | tf_op jit(solution)/shard_map/pallas_call | solution.py:482
  38.5 1.6 %copy.14 = bf16[2,32,1536]{2,1,0:T(8,128)(2,1)} copy(bf16[2,32,1536]{2,1,0:T(8,128)(2,1)} %shard_map.118) | data formatting | bytes 393216
where the time goes:
time: 40.2 us; the launch traced here: 40.1 us
  Pallas kernels  38.5 us (96%)
  local copies, waits for them, and re-layouts  1.62 us (4%)
    pallas_call x1, Pallas kernels, shards(): pl.pallas_call(functools.partial(fused, n, nx, ng, recs, frames, taps), o...  38.5 us
    unnamed x1, local copies, waits for them, and re-layouts  1.62 us

commit v1 on v0

v1 whole, which is shorter than its diff:
```python
import functools

import jax
import jax.numpy as jnp
from jax import lax
from jax.experimental import pallas as pl
from jax.experimental.pallas import tpu as pltpu
from jax.sharding import PartitionSpec as P

MESH = pl.DeviceIdType.MESH
HEAD_DIM = 64
LANES = 128
RIM = 16
W_CHUNKS = 4
epsilon = 1e-05
masked_score = -1e30
f32 = jnp.float32
bf16 = jnp.bfloat16


def swap_halves(values):
    return pltpu.roll(values, HEAD_DIM, axis=1)


def normalise(values, gain):
    centred = values - jnp.mean(values, axis=-1, keepdims=True)
    variance = jnp.mean(centred * centred, axis=-1, keepdims=True)
    return (centred * lax.rsqrt(variance + epsilon) * gain).astype(bf16)


def fused(
    n, nx, ng, recs, frames, taps,
    feat_h, counts_h, ag_h, wqkv_h, wout_h, cg_h, wglu_h, ker_h, bns_h, bnb_h, wpw_h, clip_h, out,
    feat, counts, ag, cg, ker, bns, bnb, clip,
    wqkv, wo, wglu, wpw, xn, qk_s, v_s, qk_r, v_r, atto, att_all, w_s, tot_s, parts, sibs, res, gb, gp, halo, act,
    p5, s5, sum5, x5,
    ld, sm, qs, qr, vs, vr, wos, wor, ys, yr, zs, zr, fs, fr, ss, sr, hs, hr, bs, br, es, er,
):
    c = lax.axis_index("ctx")
    m = lax.axis_index("mp")
    x = lax.div(m, 2)
    core = lax.rem(m, 2)
    g_rank = lax.axis_index("groups")
    sibling = {"mp": x * 2 + (1 - core)}
    rows, width = feat.shape
    heads = wqkv.shape[2] // HEAD_DIM
    pairs = heads // 2
    phases = recs * heads // n
    per_phase = recs // phases
    chans = gb.shape[2]
    rm = frames // (2 * nx)
    half = frames // 2

    def ctx_at(k):
        return lax.rem(c + k, n)

    def x_peer(k):
        return {"mp": lax.rem(x + k, nx) * 2 + core}

    def y_peer(k):
        return {"groups": lax.rem(g_rank + k, ng)}

    def remote(src, dst, send, recv, where):
        return pltpu.make_async_remote_copy(
            src_ref=src, dst_ref=dst, send_sem=send, recv_sem=recv, device_id=where, device_id_type=MESH
        )

    barrier = pltpu.get_barrier_semaphore()
    for k in range(1, n):
        pl.semaphore_signal(barrier, inc=1, device_id={"ctx": ctx_at(k)}, device_id_type=MESH)
    for k in range(1, nx):
        pl.semaphore_signal(barrier, inc=1, device_id=x_peer(k), device_id_type=MESH)
    for k in range(1, ng):
        pl.semaphore_signal(barrier, inc=1, device_id=y_peer(k), device_id_type=MESH)
    pl.semaphore_signal(barrier, inc=1, device_id=sibling, device_id_type=MESH)

    pairs_in = [(feat_h, feat), (ag_h, ag), (counts_h, counts), (cg_h, cg), (ker_h, ker), (bns_h, bns),
                (bnb_h, bnb), (clip_h, clip)]
    smalls = [pltpu.make_async_copy(src, dst, sm.at[i]) for i, (src, dst) in enumerate(pairs_in)]
    loads = [pltpu.make_async_copy(wqkv_h.at[i], wqkv.at[i], ld.at[i]) for i in range(3)]
    loads.append(pltpu.make_async_copy(wglu_h, wglu, ld.at[3]))
    loads.append(pltpu.make_async_copy(wpw_h, wpw, ld.at[4]))
    loads.append(pltpu.make_async_copy(wout_h, wo.at[x], ld.at[5]))
    smalls[0].start()
    smalls[1].start()
    for i in (1, 0, 2):
        loads[i].start()
    for copy in smalls[2:]:
        copy.start()
    for i in (5, 3, 4):
        loads[i].start()
    smalls[0].wait()
    smalls[1].wait()

    gain = ag[...].reshape(1, width)

    lane = lax.broadcasted_iota(jnp.int32, (1, LANES), 1)
    low = lane < HEAD_DIM

    def norm_in(f):
        def strip(i, carry):
            at = pl.ds(pl.multiple_of(f * per_phase * frames + i * 32, 32), 32)
            xn[at, :] = normalise(feat[at, :].astype(f32), gain)
            return carry

        lax.fori_loop(0, per_phase * frames // 32, strip, 0, unroll=4)

    norm_in(0)
    pl.semaphore_wait(barrier, n - 1 + nx - 1 + ng - 1 + 1)

    local = wo.shape[1]
    share = local // ng
    sub = share // W_CHUNKS

    def w_rows(rank, chunk):
        return pl.ds(pl.multiple_of(rank * share + chunk * sub, sub), sub)

    w_copies = {}
    for chunk in range(W_CHUNKS):
        for k in range(1, nx):
            at = w_rows(g_rank, chunk)
            copy = remote(wout_h.at[at, :], wo.at[x, at, :], wos.at[k, chunk], wor.at[k, chunk], x_peer(k))
            copy.start()
            w_copies[k, chunk] = copy
    y_copies = []

    def hand_on(chunk):
        for k in range(1, nx):
            w_copies[k, chunk].wait_recv()
            at = w_rows(g_rank, chunk)
            held = wo.at[lax.rem(x - k + nx, nx), at, :]
            for j in range(1, ng):
                copy = remote(held, held, ys.at[k, chunk, j], yr.at[k, chunk, j], y_peer(j))
                copy.start()
                y_copies.append(copy)

    def rows_of(rec):
        return pl.ds(rec * frames, frames)

    def columns(values, p):
        return values[:, p * LANES : (p + 1) * LANES]

    def send_units(f, src, dst, send, recv):
        copies = []
        for k in range(1, n):
            dest = ctx_at(k)
            copy = remote(src.at[f * n + dest], dst.at[f, c], send.at[f, k], recv.at[f, k], {"ctx": dest})
            copy.start()
            copies.append(copy)
        dst[f, c] = src[f * n + c]
        return copies

    qk_copies = []
    v_copies = []
    for f in range(phases):
        if f > 0:
            norm_in(f)
        if f == 0:
            loads[1].wait()
            loads[0].wait()
        mine = range(f * per_phase, (f + 1) * per_phase)
        for rec in mine:
            keys = jnp.dot(xn[rows_of(rec), :], wqkv[1], preferred_element_type=f32)
            queries = jnp.dot(xn[rows_of(rec), :], wqkv[0], preferred_element_type=f32)
            for p in range(pairs):
                q, k = columns(queries, p), columns(keys, p)
                qk_s[rec * heads + 2 * p] = jnp.where(low, q, swap_halves(k)).astype(bf16)
                qk_s[rec * heads + 2 * p + 1] = jnp.where(low, swap_halves(q), k).astype(bf16)
        qk_copies.append(send_units(f, qk_s, qk_r, qs, qr))
        if f == 0:
            loads[2].wait()
        for rec in mine:
            made = jnp.dot(xn[rows_of(rec), :], wqkv[2], preferred_element_type=f32)
            for p in range(pairs):
                v = columns(made, p)
                v_s[rec * heads + 2 * p] = jnp.where(low, v[:half], swap_halves(v[half:])).astype(bf16)
                v_s[rec * heads + 2 * p + 1] = jnp.where(low, swap_halves(v[:half]), v[half:]).astype(bf16)
        v_copies.append(send_units(f, v_s, v_r, vs, vr))

    key_count = n * frames
    slots = w_s.shape[0]
    starts = list(range(0, n, 2))

    def weigh(f, k0, slot):
        both = qk_r[f].reshape(key_count, LANES)
        keys = swap_halves(both.astype(f32)).astype(bf16)
        queries = jnp.concatenate([qk_r[f, ctx_at(k0)], qk_r[f, ctx_at(k0 + 1)]], axis=0)
        queries = jnp.where(low, queries, jnp.zeros((), bf16))
        scores = lax.dot_general(queries, keys, (((1,), (1,)), ((), ())), preferred_element_type=f32)
        live_keys = counts[lax.div(f * n + c, heads)]
        seen = lax.broadcasted_iota(jnp.int32, (1, key_count), 1) < live_keys
        scores = jnp.where(seen, scores, masked_score)
        top = jnp.max(scores, axis=-1, keepdims=True)
        weights = jnp.exp((scores - top) * (HEAD_DIM**-0.5))
        tot_s[slot] = jnp.sum(weights, axis=-1, keepdims=True)
        w_s[slot] = weights.astype(bf16)

    def mix(f, k0, slot):
        folded = v_r[f].astype(f32)
        late = swap_halves(folded.reshape(n * half, LANES)).reshape(n, half, LANES)
        values = jnp.concatenate([folded, late], axis=1).reshape(key_count, LANES).astype(bf16)
        mixed = jnp.dot(w_s[slot], values, preferred_element_type=f32) / tot_s[slot]
        for i in range(2):
            piece = mixed[i * frames : (i + 1) * frames]
            atto[f, k0 + i] = jnp.where(low, piece[:half], swap_halves(piece[half:])).astype(bf16)

    z_copies = [
        [
            remote(atto.at[f, k], att_all.at[x, f * n + c], zs.at[f, k], zr.at[f, k], {"ctx": ctx_at(k)})
            for k in range(1, n)
        ]
        for f in range(phases)
    ]

    def give(f, k):
        if k == 0:
            att_all[x, f * n + c] = atto[f, 0]
        else:
            z_copies[f][k - 1].start()

    f_copies = [[] for f in range(phases)]

    def forward(f):
        for k in range(n):
            spot = f * n + lax.rem(c - k + n, n)
            if k > 0:
                z_copies[f][k - 1].wait_recv()
            for j in range(1, nx):
                held = att_all.at[x, spot]
                copy = remote(held, held, fs.at[j, f, k], fr.at[j, f, k], x_peer(j))
                copy.start()
                f_copies[f].append(copy)

    chunks = list(range(W_CHUNKS))
    hand_on(chunks.pop(0))
    hand_on(chunks.pop(0))
    smalls[2].wait()
    for f in range(phases):
        for copy in qk_copies[f]:
            copy.wait_recv()
        if slots > 1:
            for slot, k0 in enumerate(starts):
                weigh(f, k0, slot)
        if f > 0:
            forward(f - 1)
        elif chunks:
            hand_on(chunks.pop(0))
        for copy in v_copies[f]:
            copy.wait_recv()
        if slots > 1:
            for slot, k0 in enumerate(starts):
                mix(f, k0, slot)
                give(f, k0 + 1)
                give(f, k0)
        else:
            def whole_step(i, carry, f=f):
                weigh(f, 2 * i, 0)
                mix(f, 2 * i, 0)
                return carry

            lax.fori_loop(0, n // 2, whole_step, 0)
            for k in range(n):
                give(f, k)
        while chunks:
            hand_on(chunks.pop(0))

    for copy in smalls[3:]:
        copy.wait()
    conv_gain = cg[...].reshape(1, width)

    def unfold(i, unit, odd):
        piece = att_all[i, unit].astype(f32)
        turned = swap_halves(piece)
        return jnp.concatenate([turned, piece] if odd else [piece, turned], axis=0)

    s_copies = {}

    def project_out(rec):
        gathered = jnp.concatenate(
            [
                jnp.where(
                    low, unfold(i, rec * heads + 2 * p, False), unfold(i, rec * heads + 2 * p + 1, True)
                ).astype(bf16)
                for i in range(nx)
                for p in range(pairs)
            ],
            axis=1,
        )
        parts[rec] = jnp.dot(
            gathered, wo[...].reshape(nx * pairs * LANES, width), preferred_element_type=f32
        ).astype(bf16)
        s_copies[rec] = remote(parts.at[rec], sibs.at[rec], ss.at[rec], sr.at[rec], sibling)
        s_copies[rec].start()

    first_frame = c * frames
    frame_ids = first_frame + lax.broadcasted_iota(jnp.int32, (frames, 1), 0)

    def up(rec):
        return remote(
            gb.at[rec, frames - RIM : frames, :], halo.at[0, rec], hs.at[0, rec], hr.at[0, rec],
            {"ctx": lax.rem(c + 1, n)},
        )

    def down(rec):
        return remote(
            gb.at[rec, 0:RIM, :], halo.at[1, rec], hs.at[1, rec], hr.at[1, rec], {"ctx": lax.rem(c + n - 1, n)}
        )


    def gate(rec):
        s_copies[rec].wait_recv()

        def strip(i, carry):
            near = pl.ds(pl.multiple_of(i * 32, 32), 32)
            at = pl.ds(pl.multiple_of(rec * frames + i * 32, 32), 32)
            total = feat[at, :].astype(f32) + (parts[rec, near, :].astype(f32) + sibs[rec, near, :].astype(f32))
            res[at, :] = total
            xn[at, :] = normalise(total, conv_gain)
            return carry

        lax.fori_loop(0, frames // 32, strip, 0, unroll=4)
        value_half = jnp.dot(xn[rows_of(rec), :], wglu[0], preferred_element_type=f32)
        gate_half = jnp.dot(xn[rows_of(rec), :], wglu[1], preferred_element_type=f32)
        gated = value_half * jax.nn.sigmoid(gate_half)
        kept = jnp.where(frame_ids < counts[rec], gated, 0.0).astype(bf16)
        gb[rec] = kept
        gp[rec, RIM : RIM + frames, :] = kept.astype(f32)

        @pl.when(c < n - 1)
        def _():
            up(rec).start()

        @pl.when(c > 0)
        def _():
            down(rec).start()

    scale = bns[...].reshape(1, chans)
    shift = bnb[...].reshape(1, chans)

    def depthwise(rec, start, count):
        for lo in range(0, chans, LANES):
            hi = min(lo + LANES, chans)
            total = jnp.zeros((count, hi - lo), f32)
            for tap in range(taps):
                begin = start + tap + RIM - taps // 2
                total = total + gp[rec, begin : begin + count, lo:hi] * ker[tap : tap + 1, lo:hi]
            v = total * scale[:, lo:hi] + shift[:, lo:hi]
            act[rec, start : start + count, lo:hi] = (v * jax.nn.sigmoid(v)).astype(bf16)

    def rim(rec):
        @pl.when(c > 0)
        def _():
            up(rec).wait_recv()

        @pl.when(c == 0)
        def _():
            halo[0, rec] = jnp.zeros(halo.shape[2:], bf16)

        @pl.when(c < n - 1)
        def _():
            down(rec).wait_recv()

        @pl.when(c == n - 1)
        def _():
            halo[1, rec] = jnp.zeros(halo.shape[2:], bf16)

        gp[rec, 0:RIM, :] = halo[0, rec].astype(f32)
        gp[rec, RIM + frames : 2 * RIM + frames, :] = halo[1, rec].astype(f32)
        depthwise(rec, 0, RIM)
        depthwise(rec, frames - RIM, RIM)

    b_copies = []
    e_copies = []

    def pass_on(rec):
        b_copies[rec].wait_recv()
        for i in range(nx):
            sum5[rec, i] = (p5[rec, i, core].astype(f32) + s5[rec, i].astype(f32)).astype(bf16)
        for k in range(1, nx):
            copy = remote(sum5.at[rec, lax.rem(x + k, nx)], x5.at[rec, k], es.at[rec, k], er.at[rec, k], x_peer(k))
            copy.start()
            e_copies.append(copy)

    def interior(rec):
        depthwise(rec, RIM, frames - 2 * RIM)

    loads[5].wait()
    loads[3].wait()
    for copy in y_copies:
        copy.wait_recv()
    early = list(range((phases - 1) * per_phase))
    late = list(range((phases - 1) * per_phase, recs))
    for f in range(phases - 1):
        for copy in f_copies[f]:
            copy.wait_recv()
    for rec in early:
        project_out(rec)
    forward(phases - 1)
    for rec in early:
        gate(rec)
    for copy in f_copies[phases - 1]:
        copy.wait_recv()
    for rec in late:
        project_out(rec)
    for rec in early:
        interior(rec)
    for rec in late:
        gate(rec)
    loads[4].wait()
    for rec in range(recs):
        if rec in late:
            interior(rec)
        rim(rec)
        if rec > 0:
            pass_on(rec - 1)
        made = jnp.dot(act[rec], wpw[...], preferred_element_type=f32)
        p5[rec] = made.reshape(nx, 2, rm, width).astype(bf16)
        copy = remote(p5.at[rec, :, 1 - core], s5.at[rec], bs.at[rec], br.at[rec], sibling)
        copy.start()
        b_copies.append(copy)
    pass_on(recs - 1)

    row_start = pl.multiple_of(m * rm, rm)
    mine_ids = first_frame + row_start + lax.broadcasted_iota(jnp.int32, (rm, 1), 0)
    bound = clip[...].reshape(1, width).astype(f32) / 16.0
    for rec in range(recs):
        for k in range(1, nx):
            e_copies[rec * (nx - 1) + k - 1].wait_recv()
        at = pl.ds(pl.multiple_of(rec * frames + row_start, rm), rm)
        total = res[at, :] + sum5[rec, x].astype(f32)
        for k in range(1, nx):
            total = total + x5[rec, k].astype(f32)
        clipped = jnp.minimum(jnp.maximum(total, -bound), bound)
        out[rec] = jnp.where(mine_ids < counts[rec], clipped, 0.0).astype(bf16)

    waiting = list(w_copies.values()) + y_copies + list(s_copies.values()) + b_copies + e_copies
    for group in qk_copies + v_copies + z_copies + f_copies:
        waiting = waiting + group
    for copy in waiting:
        copy.wait_send()
    for rec in range(recs):
        @pl.when(c < n - 1)
        def _(rec=rec):
            up(rec).wait_send()

        @pl.when(c > 0)
        def _(rec=rec):
            down(rec).wait_send()


def shards(n, mp, ng, features, frame_counts, attn_gain, w_qkv, w_out, conv_gain, w_glu, kernel, bn_scale, bn_shift, w_pw, clip_level):
    recs, frames, width = features.shape
    nx = mp // 2
    rows = recs * frames
    local = w_qkv.shape[2]
    units = recs * local // HEAD_DIM
    phases = units // n
    half = frames // 2
    chans = w_glu.shape[2]
    rm = frames // mp
    taps = kernel.shape[0]
    vmem = pl.BlockSpec(memory_space=pltpu.VMEM)
    hbm = pl.BlockSpec(memory_space=pl.ANY)
    dma = pltpu.SemaphoreType.DMA
    slots = n // 2 if n <= 4 else 1
    scratch = [
        pltpu.VMEM((rows, width), bf16),
        pltpu.SMEM(frame_counts.shape, jnp.int32),
        pltpu.VMEM(attn_gain.shape, f32),
        pltpu.VMEM(conv_gain.shape, f32),
        pltpu.VMEM(kernel.shape, f32),
        pltpu.VMEM(bn_scale.shape, f32),
        pltpu.VMEM(bn_shift.shape, f32),
        pltpu.VMEM(clip_level.shape, jnp.int32),
        pltpu.VMEM(w_qkv.shape, bf16),
        pltpu.VMEM((nx, local, width), bf16),
        pltpu.VMEM(w_glu.shape, bf16),
        pltpu.VMEM(w_pw.shape, bf16),
        pltpu.VMEM((rows, width), bf16),
        pltpu.VMEM((units, frames, LANES), bf16),
        pltpu.VMEM((units, half, LANES), bf16),
        pltpu.VMEM((phases, n, frames, LANES), bf16),
        pltpu.VMEM((phases, n, half, LANES), bf16),
        pltpu.VMEM((phases, n, half, LANES), bf16),
        pltpu.VMEM((nx, units, half, LANES), bf16),
        pltpu.VMEM((slots, 2 * frames, n * frames), bf16),
        pltpu.VMEM((slots, 2 * frames, 1), f32),
        pltpu.VMEM((recs, frames, width), bf16),
        pltpu.VMEM((recs, frames, width), bf16),
        pltpu.VMEM((rows, width), f32),
        pltpu.VMEM((recs, frames, chans), bf16),
        pltpu.VMEM((recs, frames + 2 * RIM, chans), f32),
        pltpu.VMEM((2, recs, RIM, chans), bf16),
        pltpu.VMEM((recs, frames, chans), bf16),
        pltpu.VMEM((recs, nx, 2, rm, width), bf16),
        pltpu.VMEM((recs, nx, rm, width), bf16),
        pltpu.VMEM((recs, nx, rm, width), bf16),
        pltpu.VMEM((recs, nx, rm, width), bf16),
        dma((6,)),
        dma((8,)),
        dma((phases, n)), dma((phases, n)),
        dma((phases, n)), dma((phases, n)),
        dma((nx, W_CHUNKS)), dma((nx, W_CHUNKS)),
        dma((nx, W_CHUNKS, ng)), dma((nx, W_CHUNKS, ng)),
        dma((phases, n)), dma((phases, n)),
        dma((nx, phases, n)), dma((nx, phases, n)),
        dma((recs,)), dma((recs,)),
        dma((2, recs)), dma((2, recs)),
        dma((recs,)), dma((recs,)),
        dma((recs, nx)), dma((recs, nx)),
    ]
    return pl.pallas_call(
        functools.partial(fused, n, nx, ng, recs, frames, taps),
        out_shape=jax.ShapeDtypeStruct((recs, rm, width), bf16),
        in_specs=[hbm] * 12,
        out_specs=vmem,
        scratch_shapes=scratch,
        compiler_params=pltpu.CompilerParams(
            collective_id=0, has_side_effects=True, vmem_limit_bytes=56 * 2**20
        ),
    )(
        features.reshape(rows, width), frame_counts, attn_gain, w_qkv, w_out, conv_gain, w_glu, kernel,
        bn_scale, bn_shift, w_pw, clip_level,
    )


def solution(mesh):
    return jax.shard_map(
        functools.partial(shards, mesh.shape["ctx"], mesh.shape["mp"], mesh.shape["groups"]),
        mesh=mesh,
        in_specs=(
            P("groups", "ctx", None),
            P("groups"),
            P(),
            P(None, None, "mp"),
            P("mp", None),
            P(),
            P(None, None, "mp"),
            P(None, "mp"),
            P("mp"),
            P("mp"),
            P("mp", None),
            P(),
        ),
        out_specs=P("groups", ("ctx", "mp"), None),
        check_vma=False,
    )
```

time: 40.2 us -> 41.4 us (1.030)
  Pallas kernels: 38.5 us -> 39.6 us
    pallas_call x1, Pallas kernels: 38.5 us -> 39.6 us  [shards(): pl.pallas_call(functools.partial(fused, n, nx, ng, recs, frames, taps), o...]
where the time goes in v1:
time: 41.4 us; the launch traced here: 41.2 us
  Pallas kernels  39.6 us (96%)
  local copies, waits for them, and re-layouts  1.62 us (4%)
    pallas_call x1, Pallas kernels, shards(): pl.pallas_call(functools.partial(fused, n, nx, ng, recs, frames, taps), o...  39.6 us
    unnamed x1, local copies, waits for them, and re-layouts  1.62 us

profile of v1, /device:TPU:0, one launch (start us, length us, event | category | flops | bytes accessed | tf_op | source)
XLA Modules:
  0.0 41.2 jit_solution(11450601718983751409)
XLA Ops:
  0.0 39.6 %shard_map.118 = bf16[2,32,1536]{2,1,0:T(8,128)(2,1)} custom-call(bf16[256,1536]{1,0:T(8,128)(2,1)} %bitcast.1, s32[2]{0:T(128)} %counts_h.1, f32[1536]{0:T(1024)} %ag_h.1, bf16[3,1536,256]{2,1,0:T(8,128)(2,1)} %wqkv_h.1, bf16[256,1536]{1,0:T(8,128)(2,1)} %wout_h.1, f32[1536]{0:T(1024)} %cg_h.1, bf16[2,1536,384]{2,1,0:T(8,128)(2,1)} %wglu_h.1, ...), custom_call_target="tpu_custom_call" | custom-call | tf_op jit(solution)/shard_map/pallas_call | solution.py:512
  39.6 1.6 %copy.14 = bf16[2,32,1536]{2,1,0:T(8,128)(2,1)} copy(bf16[2,32,1536]{2,1,0:T(8,128)(2,1)} %shard_map.118) | data formatting | bytes 393216

commit v2 on v1

--- a/solution.py
+++ b/solution.py
@@ -87,8 +87,6 @@
         loads[i].start()
     for copy in smalls[2:]:
         copy.start()
-    for i in (5, 3, 4):
-        loads[i].start()
     smalls[0].wait()
     smalls[1].wait()
 
@@ -97,15 +95,12 @@
     lane = lax.broadcasted_iota(jnp.int32, (1, LANES), 1)
     low = lane < HEAD_DIM
 
-    def norm_in(f):
-        def strip(i, carry):
-            at = pl.ds(pl.multiple_of(f * per_phase * frames + i * 32, 32), 32)
-            xn[at, :] = normalise(feat[at, :].astype(f32), gain)
-            return carry
-
-        lax.fori_loop(0, per_phase * frames // 32, strip, 0, unroll=4)
-
-    norm_in(0)
+    def norm_in(i, carry):
+        at = pl.ds(pl.multiple_of(i * 32, 32), 32)
+        xn[at, :] = normalise(feat[at, :].astype(f32), gain)
+        return carry
+
+    lax.fori_loop(0, rows // 32, norm_in, 0, unroll=2)
     pl.semaphore_wait(barrier, n - 1 + nx - 1 + ng - 1 + 1)
 
     local = wo.shape[1]
@@ -135,47 +130,49 @@
                 y_copies.append(copy)
 
     def rows_of(rec):
-        return pl.ds(rec * frames, frames)
+        return pl.ds(pl.multiple_of(rec * frames, frames), frames)
 
     def columns(values, p):
         return values[:, p * LANES : (p + 1) * LANES]
 
-    def send_units(f, src, dst, send, recv):
-        copies = []
-        for k in range(1, n):
-            dest = ctx_at(k)
-            copy = remote(src.at[f * n + dest], dst.at[f, c], send.at[f, k], recv.at[f, k], {"ctx": dest})
-            copy.start()
-            copies.append(copy)
-        dst[f, c] = src[f * n + c]
-        return copies
-
-    qk_copies = []
-    v_copies = []
-    for f in range(phases):
-        if f > 0:
-            norm_in(f)
-        if f == 0:
-            loads[1].wait()
-            loads[0].wait()
-        mine = range(f * per_phase, (f + 1) * per_phase)
-        for rec in mine:
+    def unit_copies(f, src, dst, send, recv):
+        return [
+            remote(src.at[f * n + ctx_at(k)], dst.at[f, c], send.at[f, k], recv.at[f, k], {"ctx": ctx_at(k)})
+            for k in range(1, n)
+        ]
+
+    for i in range(3):
+        loads[i].wait()
+
+    def make_units(f, carry):
+        for r in range(per_phase):
+            rec = f * per_phase + r
             keys = jnp.dot(xn[rows_of(rec), :], wqkv[1], preferred_element_type=f32)
             queries = jnp.dot(xn[rows_of(rec), :], wqkv[0], preferred_element_type=f32)
             for p in range(pairs):
                 q, k = columns(queries, p), columns(keys, p)
                 qk_s[rec * heads + 2 * p] = jnp.where(low, q, swap_halves(k)).astype(bf16)
                 qk_s[rec * heads + 2 * p + 1] = jnp.where(low, swap_halves(q), k).astype(bf16)
-        qk_copies.append(send_units(f, qk_s, qk_r, qs, qr))
-        if f == 0:
-            loads[2].wait()
-        for rec in mine:
+        for copy in unit_copies(f, qk_s, qk_r, qs, qr):
+            copy.start()
+        qk_r[f, c] = qk_s[f * n + c]
+        for r in range(per_phase):
+            rec = f * per_phase + r
             made = jnp.dot(xn[rows_of(rec), :], wqkv[2], preferred_element_type=f32)
             for p in range(pairs):
                 v = columns(made, p)
                 v_s[rec * heads + 2 * p] = jnp.where(low, v[:half], swap_halves(v[half:])).astype(bf16)
                 v_s[rec * heads + 2 * p + 1] = jnp.where(low, swap_halves(v[:half]), v[half:]).astype(bf16)
-        v_copies.append(send_units(f, v_s, v_r, vs, vr))
+        for copy in unit_copies(f, v_s, v_r, vs, vr):
+            copy.start()
+        v_r[f, c] = v_s[f * n + c]
+        return carry
+
+    lax.fori_loop(0, phases, make_units, 0)
+    qk_copies = [unit_copies(f, qk_s, qk_r, qs, qr) for f in range(phases)]
+    v_copies = [unit_copies(f, v_s, v_r, vs, vr) for f in range(phases)]
+    for i in (5, 3, 4):
+        loads[i].start()
 
     key_count = n * frames
     slots = w_s.shape[0]
@@ -239,8 +236,7 @@
         for copy in qk_copies[f]:
             copy.wait_recv()
         if slots > 1:
-            for slot, k0 in enumerate(starts):
-                weigh(f, k0, slot)
+            lax.fori_loop(0, slots, lambda i, carry, f=f: (weigh(f, 2 * i, i), carry)[1], 0)
         if f > 0:
             forward(f - 1)
         elif chunks:
@@ -318,7 +314,7 @@
             xn[at, :] = normalise(total, conv_gain)
             return carry
 
-        lax.fori_loop(0, frames // 32, strip, 0, unroll=4)
+        lax.fori_loop(0, frames // 32, strip, 0, unroll=2)
         value_half = jnp.dot(xn[rows_of(rec), :], wglu[0], preferred_element_type=f32)
         gate_half = jnp.dot(xn[rows_of(rec), :], wglu[1], preferred_element_type=f32)
         gated = value_half * jax.nn.sigmoid(gate_half)
@@ -334,18 +330,22 @@
         def _():
             down(rec).start()
 
-    scale = bns[...].reshape(1, chans)
-    shift = bnb[...].reshape(1, chans)
-
-    def depthwise(rec, start, count):
-        for lo in range(0, chans, LANES):
-            hi = min(lo + LANES, chans)
-            total = jnp.zeros((count, hi - lo), f32)
+    def depthwise(rec):
+        def channels(at, size):
+            total = jnp.zeros((frames, size), f32)
             for tap in range(taps):
-                begin = start + tap + RIM - taps // 2
-                total = total + gp[rec, begin : begin + count, lo:hi] * ker[tap : tap + 1, lo:hi]
-            v = total * scale[:, lo:hi] + shift[:, lo:hi]
-            act[rec, start : start + count, lo:hi] = (v * jax.nn.sigmoid(v)).astype(bf16)
+                begin = tap + RIM - taps // 2
+                total = total + gp[rec, begin : begin + frames, at] * ker[tap : tap + 1, at]
+            v = total * bns[at].reshape(1, size) + bnb[at].reshape(1, size)
+            act[rec, :, at] = (v * jax.nn.sigmoid(v)).astype(bf16)
+
+        def step(j, carry):
+            channels(pl.ds(pl.multiple_of(j * LANES, LANES), LANES), LANES)
+            return carry
+
+        lax.fori_loop(0, chans // LANES, step, 0)
+        if chans % LANES:
+            channels(pl.ds(chans - chans % LANES, chans % LANES), chans % LANES)
 
     def rim(rec):
         @pl.when(c > 0)
@@ -366,8 +366,7 @@
 
         gp[rec, 0:RIM, :] = halo[0, rec].astype(f32)
         gp[rec, RIM + frames : 2 * RIM + frames, :] = halo[1, rec].astype(f32)
-        depthwise(rec, 0, RIM)
-        depthwise(rec, frames - RIM, RIM)
+        depthwise(rec)
 
     b_copies = []
     e_copies = []
@@ -380,9 +379,6 @@
             copy = remote(sum5.at[rec, lax.rem(x + k, nx)], x5.at[rec, k], es.at[rec, k], er.at[rec, k], x_peer(k))
             copy.start()
             e_copies.append(copy)
-
-    def interior(rec):
-        depthwise(rec, RIM, frames - 2 * RIM)
 
     loads[5].wait()
     loads[3].wait()
@@ -402,14 +398,10 @@
         copy.wait_recv()
     for rec in late:
         project_out(rec)
-    for rec in early:
-        interior(rec)
     for rec in late:
         gate(rec)
     loads[4].wait()
     for rec in range(recs):
-        if rec in late:
-            interior(rec)
         rim(rec)
         if rec > 0:
             pass_on(rec - 1)

time: 41.4 us -> 42.2 us (1.019)
  Pallas kernels: 39.6 us -> 40.5 us
    pallas_call x1, Pallas kernels: 39.6 us -> 40.5 us  [shards(): pl.pallas_call(functools.partial(fused, n, nx, ng, recs, frames, taps), o...]
where the time goes in v2:
time: 42.2 us; the launch traced here: 42.1 us
  Pallas kernels  40.5 us (96%)
  local copies, waits for them, and re-layouts  1.62 us (4%)
    pallas_call x1, Pallas kernels, shards(): pl.pallas_call(functools.partial(fused, n, nx, ng, recs, frames, taps), o...  40.5 us
    unnamed x1, local copies, waits for them, and re-layouts  1.62 us

profile of v2, /device:TPU:0, one launch (start us, length us, event | category | flops | bytes accessed | tf_op | source)
XLA Modules:
  0.0 42.1 jit_solution(938586944084288581)
XLA Ops:
  0.0 40.5 %shard_map.118 = bf16[2,32,1536]{2,1,0:T(8,128)(2,1)} custom-call(bf16[256,1536]{1,0:T(8,128)(2,1)} %bitcast.1, s32[2]{0:T(128)} %counts_h.1, f32[1536]{0:T(1024)} %ag_h.1, bf16[3,1536,256]{2,1,0:T(8,128)(2,1)} %wqkv_h.1, bf16[256,1536]{1,0:T(8,128)(2,1)} %wout_h.1, f32[1536]{0:T(1024)} %cg_h.1, bf16[2,1536,384]{2,1,0:T(8,128)(2,1)} %wglu_h.1, ...), custom_call_target="tpu_custom_call" | custom-call | tf_op jit(solution)/shard_map/pallas_call | solution.py:504
  40.5 1.6 %copy.14 = bf16[2,32,1536]{2,1,0:T(8,128)(2,1)} copy(bf16[2,32,1536]{2,1,0:T(8,128)(2,1)} %shard_map.118) | data formatting | bytes 393216

commit v3 on v0

--- a/solution.py
+++ b/solution.py
@@ -40,7 +40,7 @@
 
 def fused(
     n, nx, ng, recs, frames, taps,
-    feat_h, counts_h, ag_h, wqkv_h, wout_h, cg_h, wglu_h, ker_h, bns_h, bnb_h, wpw_h, clip_h, out,
+    feat_h, counts_h, ag_h, wqkv_h, wout_h, cg_h, wglu_h, ker_h, bns_h, bnb_h, wpw_h, clip_h, out, least, most,
     feat, counts, ag, cg, ker, bns, bnb, clip,
     wqkv, wo, wglu, wpw, xn, qkv_s, qkv_r, atto, att_all, w_s, tot_s, parts, sibs, res, gb, gp, halo, act,
     p5, s5, sum5, x5,
@@ -99,8 +99,6 @@
         loads[i].start()
     for copy in smalls[2:]:
         copy.start()
-    for i in (5, 3, 4):
-        loads[i].start()
     smalls[0].wait()
     smalls[1].wait()
 
@@ -170,6 +168,8 @@
         for k in range(1, n)
     ]
 
+    for i in (5, 3, 4):
+        loads[i].start()
     hand_on(0)
     smalls[2].wait()
 
@@ -245,7 +245,7 @@
                 give(k)
 
     f_copies = []
-    for k in range(n):
+    for k in [0] + list(range(n - 1, 0, -1)):
         unit = lax.rem(c - k + n, n)
         spot = lax.rem(unit, units)
 
@@ -328,6 +328,9 @@
 
     for copy in smalls[4:]:
         copy.wait()
+    bound = clip[...].astype(f32) / 16.0
+    least[...] = -bound
+    most[...] = bound
     scale = bns[...].reshape(1, chans)
     shift = bnb[...].reshape(1, chans)
 
@@ -390,7 +393,6 @@
 
     row_start = pl.multiple_of(m * rm, rm)
     mine_ids = first_frame + row_start + lax.broadcasted_iota(jnp.int32, (rm, 1), 0)
-    bound = clip[...].reshape(1, width).astype(f32) / 16.0
     for rec in range(recs):
         for k in range(1, nx):
             e_copies[rec * (nx - 1) + k - 1].wait_recv()
@@ -398,8 +400,7 @@
         total = res[at, :] + sum5[rec, x].astype(f32)
         for k in range(1, nx):
             total = total + x5[rec, k].astype(f32)
-        clipped = jnp.minimum(jnp.maximum(total, -bound), bound)
-        out[rec] = jnp.where(mine_ids < counts[rec], clipped, 0.0).astype(bf16)
+        out[rec] = jnp.where(mine_ids < counts[rec], total, 0.0).astype(bf16)
 
     for copy, dest, _i in q_copies:
         when(has_unit(dest))(copy.wait_send)
@@ -479,11 +480,15 @@
         dma((recs,)), dma((recs,)),
         dma((recs, nx)), dma((recs, nx)),
     ]
-    return pl.pallas_call(
+    summed, least, most = pl.pallas_call(
         functools.partial(fused, n, nx, ng, recs, frames, taps),
-        out_shape=jax.ShapeDtypeStruct((recs, rm, width), bf16),
+        out_shape=(
+            jax.ShapeDtypeStruct((recs, rm, width), bf16),
+            jax.ShapeDtypeStruct((width,), f32),
+            jax.ShapeDtypeStruct((width,), f32),
+        ),
         in_specs=[hbm] * 12,
-        out_specs=vmem,
+        out_specs=(vmem, vmem, vmem),
         scratch_shapes=scratch,
         compiler_params=pltpu.CompilerParams(
             collective_id=0, has_side_effects=True, vmem_limit_bytes=56 * 2**20
@@ -492,6 +497,7 @@
         features.reshape(rows, width), frame_counts, attn_gain, w_qkv, w_out, conv_gain, w_glu, kernel,
         bn_scale, bn_shift, w_pw, clip_level,
     )
+    return jnp.clip(summed.astype(f32), least, most).astype(bf16)
 
 
 def solution(mesh):

time: 40.2 us -> 40.1 us (level)
  other arithmetic: 0 us -> 1.67 us
  local copies, waits for them, and re-layouts: 1.62 us -> 0 us
    convert_element_type x0 -> x1, other arithmetic: none -> 1.67 us  [shards(): return jnp.clip(summed.astype(f32), least, most).astype(bf16)]
    unnamed x1 -> x0, local copies, waits for them, and re-layouts: 1.62 us -> none
where the time goes in v3:
time: 40.1 us; the launch traced here: 40 us
  Pallas kernels  38.3 us (96%)
  other arithmetic  1.67 us (4%)
    pallas_call x1, Pallas kernels, shards(): pl.pallas_call(functools.partial(fused, n, nx, ng, recs, frames, taps), o...  38.3 us
    convert_element_type x1, other arithmetic, shards(): return jnp.clip(summed.astype(f32), least, most).astype(bf16)  1.67 us

profile of v3, /device:TPU:0, one launch (start us, length us, event | category | flops | bytes accessed | tf_op | source)
XLA Modules:
  0.0 40.0 jit_solution(1054842085385623664)
XLA Ops:
  0.0 38.3 %shard_map.118 = (bf16[2,32,1536]{2,1,0:T(8,128)(2,1)}, f32[1536]{0:T(1024)}, f32[1536]{0:T(1024)}) custom-call(bf16[256,1536]{1,0:T(8,128)(2,1)} %bitcast.1, s32[2]{0:T(128)} %counts_h.1, f32[1536]{0:T(1024)} %ag_h.1, bf16[3,1536,256]{2,1,0:T(8,128)(2,1)} %wqkv_h.1, bf16[256,1536]{1,0:T(8,128)(2,1)} %wout_h.1, f32[1536]{0:T(1024)} %cg_h.1, ...), custom_call_target="tpu_custom_call" | custom-call | tf_op jit(solution)/shard_map/pallas_call | solution.py:483
  38.3 1.7 %minimum_convert_fusion = bf16[2,32,1536]{2,1,0:T(8,128)(2,1)} fusion(bf16[2,32,1536]{2,1,0:T(8,128)(2,1)} %get-tuple-element.10, f32[1536]{0:T(1024)} %get-tuple-element.9, f32[1536]{0:T(1024)} %get-tuple-element.8), kind=kLoop, calls=%fused_computation | loop fusion | flops 589824 | bytes 405504 | tf_op jit(solution)/shard_map/convert_element_type | solution.py:500

commit v4 on v3

--- a/solution.py
+++ b/solution.py
@@ -11,7 +11,7 @@
 HEAD_DIM = 64
 LANES = 128
 RIM = 16
-W_CHUNKS = 2
+W_CHUNKS = 4
 epsilon = 1e-05
 masked_score = -1e30
 f32 = jnp.float32
@@ -171,6 +171,7 @@
     for i in (5, 3, 4):
         loads[i].start()
     hand_on(0)
+    hand_on(1)
     smalls[2].wait()
 
     def arrived(which):
@@ -223,7 +224,7 @@
             for slot, k0 in enumerate(starts):
                 weigh(k0, slot)
 
-    for chunk in range(1, W_CHUNKS):
+    for chunk in range(2, W_CHUNKS):
         hand_on(chunk)
     arrived((2,))
 
@@ -374,16 +375,19 @@
             e_copies.append(copy)
 
     for rec in range(recs):
-        depthwise(rec, RIM, frames - 2 * RIM)
         if rec == 0:
+            depthwise(rec, RIM, frames - 2 * RIM)
             rim()
             loads[4].wait()
         gp[rec, 0:RIM, :] = halo[0, rec].astype(f32)
         gp[rec, RIM + frames : 2 * RIM + frames, :] = halo[1, rec].astype(f32)
-        depthwise(rec, 0, RIM)
-        depthwise(rec, frames - RIM, RIM)
-        if rec > 0:
+        if rec == 0:
+            depthwise(rec, 0, RIM)
+            depthwise(rec, frames - RIM, RIM)
+        else:
+            depthwise(rec, 0, frames // 2)
             pass_on(rec - 1)
+            depthwise(rec, frames // 2, frames // 2)
         made = jnp.dot(act[rec], wpw[...], preferred_element_type=f32)
         p5[rec] = made.reshape(nx, 2, rm, width).astype(bf16)
         copy = remote(p5.at[rec, :, 1 - core], s5.at[rec], bs.at[rec], br.at[rec], sibling)

time: 40.1 us -> 40.6 us (1.012)
    pallas_call x1, Pallas kernels: 38.3 us -> 38.7 us  [shards(): pl.pallas_call(functools.partial(fused, n, nx, ng, recs, frames, taps), o...]
where the time goes in v4:
time: 40.6 us; the launch traced here: 40.4 us
  Pallas kernels  38.7 us (95%)
  other arithmetic  1.67 us (4%)
    pallas_call x1, Pallas kernels, shards(): pl.pallas_call(functools.partial(fused, n, nx, ng, recs, frames, taps), o...  38.7 us
    convert_element_type x1, other arithmetic, shards(): return jnp.clip(summed.astype(f32), least, most).astype(bf16)  1.67 us

profile of v4, /device:TPU:0, one launch (start us, length us, event | category | flops | bytes accessed | tf_op | source)
XLA Modules:
  0.0 40.4 jit_solution(5565173263124951879)
XLA Ops:
  0.0 38.7 %shard_map.118 = (bf16[2,32,1536]{2,1,0:T(8,128)(2,1)}, f32[1536]{0:T(1024)}, f32[1536]{0:T(1024)}) custom-call(bf16[256,1536]{1,0:T(8,128)(2,1)} %bitcast.1, s32[2]{0:T(128)} %counts_h.1, f32[1536]{0:T(1024)} %ag_h.1, bf16[3,1536,256]{2,1,0:T(8,128)(2,1)} %wqkv_h.1, bf16[256,1536]{1,0:T(8,128)(2,1)} %wout_h.1, f32[1536]{0:T(1024)} %cg_h.1, ...), custom_call_target="tpu_custom_call" | custom-call | tf_op jit(solution)/shard_map/pallas_call | solution.py:487
  38.7 1.7 %minimum_convert_fusion = bf16[2,32,1536]{2,1,0:T(8,128)(2,1)} fusion(bf16[2,32,1536]{2,1,0:T(8,128)(2,1)} %get-tuple-element.10, f32[1536]{0:T(1024)} %get-tuple-element.9, f32[1536]{0:T(1024)} %get-tuple-element.8), kind=kLoop, calls=%fused_computation | loop fusion | flops 589824 | bytes 405504 | tf_op jit(solution)/shard_map/convert_element_type | solution.py:504
